TPU v7x, 32 devices: a whole 2x2x4 slice. The times are simulated.
32 devices in a mesh: cfg: 2 (over y), row: 4 (over z), col: 4 (over x, core).
Axes of the slice: x: 2, y: 2, z: 4, core: 2. Of those that a mesh axis runs over, the one named last changes fastest.
Arguments:
- sigma_top: bfloat16 [8192, 4096], P(('cfg', 'row'), 'col'), parts along dimension 0, as said below
- par_panel: bfloat16 [8, 4, 6, 128, 128], P(('cfg', 'row'), 'col'), parts along dimension 0, may hold values from -0.03125 to 0.03125
- par_list: int32 [8, 4, 6], P(('cfg', 'row')), parts along dimension 0, may hold values from 0 to 7, as said below
- child_panel: bfloat16 [16, 4, 3, 128, 128], P(('cfg', 'row'), 'col'), parts along dimension 0, may hold values from -0.046875 to 0.046875
- child_top: bfloat16 [16, 128, 128], P(('cfg', 'row')), parts along dimension 0, may hold values from -0.625 to 0.625
- child_list: int32 [16, 4, 3], P(('cfg', 'row')), parts along dimension 0, may hold values from 0 to 5, as said below
- par_inv: float32 [8, 128, 128], P(('cfg', 'row')), parts along dimension 0, as said below
- child_inv: float32 [16, 128, 128], P(('cfg', 'row')), parts along dimension 0, as said below
Outputs:
- par_column: bfloat16 [8, 4, 6, 128, 128], P(('cfg', 'row'), 'col'), parts along dimension 0
- par_var: float32 [8, 128], P(('cfg', 'row')), parts along dimension 0
- child_column: bfloat16 [16, 4, 3, 128, 128], P(('cfg', 'row'), 'col'), parts along dimension 0
- child_row: bfloat16 [16, 128, 128], P(('cfg', 'row')), parts along dimension 0
- child_var: float32 [16, 128], P(('cfg', 'row')), parts along dimension 0
There are 2 independent parts, one for each index of `cfg`. A program takes and returns all parts, laid end to end along the dimension named above; each array names one. Nothing has to cross between parts.
Inputs may be any that keep to these rules, and one draw needn't show every extreme that they name: `sigma_top`: symmetric. `par_list`: for each parent and group, 6 distinct increasing indices within the group. `child_list`: for each child and group, 3 distinct increasing slots of its parent's list in that group. `par_inv`: lower triangular. `child_inv`: lower triangular.
All inputs are finite; a program needn't handle non-finite values.
Results may differ from a plain program's by a relative error of at most 0.0052.
Values may be sent and summed in bfloat16 or wider, within the bound.
A program may use at most 64 MiB of HBM per device.

v0:
```python
import jax
import jax.numpy as jnp
from jax import lax
from jax.sharding import PartitionSpec as P

PRECISE = lax.Precision.HIGHEST


def densify(onehot_table, panel):
    spread = jnp.einsum("kqg,kqbn->gbkn", onehot_table, panel, preferred_element_type=jnp.float32)
    return spread.astype(jnp.bfloat16)


def on_device(
    sigma_top, par_panel, par_list, child_panel, child_top, child_list, par_inv, child_inv
):
    col_group = lax.axis_index("col")
    n_parents = par_panel.shape[0]
    n_children = child_panel.shape[0]
    block_width = par_panel.shape[-1]
    n_groups = par_list.shape[1]
    group_blocks = sigma_top.shape[1] // block_width
    total_blocks = n_groups * group_blocks
    slot_count = par_list.shape[2]
    child_count = child_list.shape[2]
    n_panels = n_parents + n_children
    parent_of = jnp.arange(n_children, dtype=jnp.int32) // 2
    par_here = lax.dynamic_index_in_dim(par_list, col_group, 1, keepdims=False)
    child_here = lax.dynamic_index_in_dim(child_list, col_group, 1, keepdims=False)
    child_local = jnp.take_along_axis(par_here[parent_of], child_here, axis=1)
    block_grid = jnp.arange(group_blocks, dtype=jnp.int32)
    par_onehot = (par_here[:, :, None] == block_grid).astype(jnp.bfloat16)
    child_onehot = (child_local[:, :, None] == block_grid).astype(jnp.bfloat16)
    dense_panels = jnp.concatenate(
        [densify(par_onehot, par_panel[:, 0]), densify(child_onehot, child_panel[:, 0])], axis=2
    )
    dense_panels = dense_panels.reshape(group_blocks * block_width, n_panels * block_width)
    products = jnp.dot(
        lax.all_gather(sigma_top, "row", axis=0, tiled=True),
        dense_panels,
        preferred_element_type=jnp.float32,
    ).astype(jnp.bfloat16)
    product_blocks = products.reshape(total_blocks, block_width, n_panels, block_width)
    offsets = (jnp.arange(n_groups, dtype=jnp.int32) * group_blocks)[:, None]
    par_blocks = par_list + offsets[None]
    child_blocks = jnp.take_along_axis(par_blocks[parent_of], child_list, axis=2)

    def pick_blocks(block_index, column):
        found_rows = jnp.take(product_blocks, block_index.reshape(-1), axis=0)
        return lax.dynamic_index_in_dim(found_rows, column, 2, keepdims=False)

    par_partial = jax.vmap(pick_blocks)(par_blocks, jnp.arange(n_parents, dtype=jnp.int32))
    par_partial = par_partial.reshape(n_parents, n_groups, slot_count, block_width, block_width)
    child_partial = jax.vmap(pick_blocks)(
        child_blocks, n_parents + jnp.arange(n_children, dtype=jnp.int32)
    )
    child_partial = child_partial.reshape(
        n_children, n_groups, child_count, block_width, block_width
    )
    par_gram = jnp.einsum("pji,pjk->pik", par_inv, par_inv, precision=PRECISE)
    child_gram = jnp.einsum("cji,cjk->cik", child_inv, child_inv, precision=PRECISE)
    top_wide = child_top.astype(jnp.float32)
    par_recv, child_recv = (
        lax.all_to_all(par_partial, "col", split_axis=1, concat_axis=1, tiled=True),
        lax.all_to_all(child_partial, "col", split_axis=1, concat_axis=1, tiled=True),
    )
    par_sum = jnp.sum(par_recv.astype(jnp.float32), axis=1, keepdims=True)
    child_sum = jnp.sum(child_recv.astype(jnp.float32), axis=1, keepdims=True)
    par_column = (-par_sum).astype(jnp.bfloat16)
    par_col_wide = par_column[:, 0].astype(jnp.float32)
    parent_sel = jnp.take_along_axis(par_col_wide[parent_of], child_here[:, :, None, None], axis=1)
    upper_rows = child_sum[:, 0] + jnp.einsum(
        "csbk,ckn->csbn", parent_sel, top_wide, precision=PRECISE
    )
    child_column = (-upper_rows).astype(jnp.bfloat16)[:, None]
    child_pan_wide = child_panel[:, 0].astype(jnp.float32)
    par_piece = jnp.einsum(
        "pqki,pqkn->pin", par_panel[:, 0].astype(jnp.float32), par_col_wide, precision=PRECISE
    )
    row_piece = jnp.einsum("cski,cskn->cin", parent_sel, child_pan_wide, precision=PRECISE)
    child_piece = jnp.einsum(
        "cski,cskn->cin", child_pan_wide, child_column[:, 0].astype(jnp.float32), precision=PRECISE
    )
    par_total, row_total = lax.psum((par_piece, row_piece), "col")
    par_cov = par_gram - par_total
    parent_rows = row_total + jnp.einsum(
        "cik,ckn->cin", par_cov[parent_of], top_wide, precision=PRECISE
    )
    child_total = lax.psum(child_piece.astype(jnp.bfloat16), "col").astype(jnp.float32)
    child_cov = (
        child_gram
        - child_total
        + jnp.einsum("cki,ckn->cin", top_wide, parent_rows, precision=PRECISE)
    )
    par_var = jnp.diagonal(par_cov, axis1=1, axis2=2)
    child_row = (-parent_rows).astype(jnp.bfloat16)
    child_var = jnp.diagonal(child_cov, axis1=1, axis2=2)
    return (par_column, par_var, child_column, child_row, child_var)


def solution(mesh):
    in_specs = (
        P(("cfg", "row"), "col"),
        P(("cfg", "row"), "col", None, None, None),
        P(("cfg", "row"), None, None),
        P(("cfg", "row"), "col", None, None, None),
        P(("cfg", "row"), None, None),
        P(("cfg", "row"), None, None),
        P(("cfg", "row"), None, None),
        P(("cfg", "row"), None, None),
    )
    out_specs = (
        P(("cfg", "row"), "col", None, None, None),
        P(("cfg", "row"), None),
        P(("cfg", "row"), "col", None, None, None),
        P(("cfg", "row"), None, None),
        P(("cfg", "row"), None),
    )
    return jax.shard_map(
        on_device, mesh=mesh, in_specs=in_specs, out_specs=out_specs, check_vma=False
    )
```

profile of v0, /device:TPU:0, one launch (start us, length us, event | category | flops | bytes accessed | tf_op | source)
XLA Modules:
  0.0 296.6 jit_solution(14576388076796482711)
XLA Ops:
  8.0 0.8 broadcast_add_fusion
  8.9 0.8 copy.70
  9.7 0.8 constant_dynamic-slice_fusion
  14.6 0.9 gather_fusion.5
  16.9 145.1 %all-gather.2.cloned.1.call-done = bf16[4096,1024]{1,0:T(8,128)(2,1)} async-done(((bf16[1024,1024]{1,0:T(8,128)(2,1)}), bf16[4096,1024]{1,0:T(8,128)(2,1)}) %all-gather.2.cloned.1.call-update) | async-done | bytes 8388624 | tf_op jit(solution)/shard_map/all_gather | solution.py:39
  162.0 9.2 %fusion = bf16[48,8,32,128]{3,1,2,0:T(8,128)(2,1)S(1)} fusion(bf16[4096,1024]{1,0:T(8,128)(2,1)} %all-gather.2.cloned.1.call-done, bf16[48,8,8,128]{3,2,1,0:T(8,128)(2,1)S(1)} %bitcast.129), kind=kOutput, calls=%fused_computation.10 | convolution fusion | flops 3222798336 | bytes 12320768 | tf_op jit(solution)/shard_map/dot_general | solution.py:38
  171.2 2.5 copy.104
  173.7 3.8 %copy.66 = bf16[32,128,3,128]{3,1,2,0:T(8,128)(2,1)S(1)} copy(bf16[32,128,3,128]{1,0,3,2:T(8,128)(2,1)} %bitcast.123) | data formatting | bytes 6291456 | tf_op jit(solution)/shard_map/reshape | solution.py:43
  177.5 2.4 gather_fusion
  179.9 2.2 slice_select_fusion
  182.0 4.2 %all-to-all-start = ((bf16[1,4,6,128,128]{4,3,2,0,1:T(8,128)(2,1)}), bf16[1,4,6,128,128]{4,3,2,0,1:T(8,128)(2,1)}, u32[]{:S(2)}, u32[]{:S(2)}) async-start(bf16[1,4,6,128,128]{4,3,2,0,1:T(8,128)(2,1)} %bitcast.125), calls=%async_computation | async-start | bytes 1572864 | tf_op jit(solution)/shard_map/all_to_all | solution.py:64
  186.9 1.2 compare_and_fusion
  188.1 2.4 gather_fusion.2
  190.5 2.0 copy_select_fusion
  192.4 0.7 gather_fusion.6
  193.1 1.0 copy.77
  194.1 3.9 %all-to-all-done = bf16[1,4,6,128,128]{4,3,2,0,1:T(8,128)(2,1)} async-done(((bf16[1,4,6,128,128]{4,3,2,0,1:T(8,128)(2,1)}), bf16[1,4,6,128,128]{4,3,2,0,1:T(8,128)(2,1)}, u32[]{:S(2)}, u32[]{:S(2)}) %all-to-all-start) | async-done | bytes 786464 | tf_op jit(solution)/shard_map/all_to_all | solution.py:64
  198.0 3.5 %all-to-all-start.1 = ((bf16[2,4,3,128,128]{4,3,2,0,1:T(8,128)(2,1)}), bf16[2,4,3,128,128]{4,3,2,0,1:T(8,128)(2,1)S(1)}, u32[]{:S(2)}, u32[]{:S(2)}) async-start(bf16[2,4,3,128,128]{4,3,2,0,1:T(8,128)(2,1)} %copy.77), calls=%async_computation.1 | async-start | bytes 1572864 | tf_op jit(solution)/shard_map/all_to_all | solution.py:65
  201.5 1.3 convert_reduce_fusion.1
  202.8 0.7 fusion.42
  204.4 0.9 convolution_bitcast_fusion.4
  205.3 7.8 %all-to-all-done.1 = bf16[2,4,3,128,128]{4,3,2,0,1:T(8,128)(2,1)S(1)} async-done(((bf16[2,4,3,128,128]{4,3,2,0,1:T(8,128)(2,1)}), bf16[2,4,3,128,128]{4,3,2,0,1:T(8,128)(2,1)S(1)}, u32[]{:S(2)}, u32[]{:S(2)}) %all-to-all-start.1) | async-done | bytes 786464 | tf_op jit(solution)/shard_map/all_to_all | solution.py:65
  213.8 0.9 fusion.7
  214.8 1.0 convolution_bitcast_fusion.1
  215.8 27.4 %all-reduce.4.cloned.1.call-done = bf16[2,128,128]{2,1,0:T(8,128)(2,1)} async-done(((bf16[2,128,128]{2,1,0:T(8,128)(2,1)}), bf16[2,128,128]{2,1,0:T(8,128)(2,1)}) %all-reduce.4.cloned.1.call-update) | async-done | bytes 65552 | tf_op jit(solution)/shard_map/psum | solution.py:89
  243.3 1.2 convolution_subtract_fusion
  244.5 33.6 %all-reduce.6.cloned.1.call-done = (f32[1,128,128]{2,1,0:T(8,128)}, f32[2,128,128]{2,1,0:T(8,128)}) async-done(((f32[1,128,128]{2,1,0:T(8,128)}, f32[2,128,128]{2,1,0:T(8,128)}), (f32[1,128,128]{2,1,0:T(8,128)}, f32[2,128,128]{2,1,0:T(8,128)})) %all-reduce.6.cloned.1.call-update) | async-done | bytes 196624 | tf_op jit(solution)/shard_map/psum | solution.py:84
  278.1 1.1 fusion.9
  279.2 1.7 negate_convert_fusion.1
  281.2 4.6 %copy.85 = f32[2,128,128]{0,2,1:T(8,128)} copy(f32[2,128,128]{2,1,0:T(8,128)S(1)} %fusion.5) | data formatting | bytes 262144 | tf_op jit(solution)/shard_map/add | solution.py:91
  285.9 1.8 gather_fusion.1
  287.6 1.8 gather_fusion.3
  (65 shorter events, 9.5 us)
Async XLA Ops:
  7.2 5.8 %copy-start = (bf16[2,1,3,128,128]{4,3,2,1,0:T(8,128)(2,1)S(1)}, bf16[2,1,3,128,128]{4,3,2,1,0:T(8,128)(2,1)}, u32[]{:S(2)}) copy-start(bf16[2,1,3,128,128]{4,3,2,1,0:T(8,128)(2,1)} %param.11) | copy-start | bytes 589828
  7.2 4.9 %copy-start.1 = (bf16[1,1,6,128,128]{4,3,2,1,0:T(8,128)(2,1)S(1)}, bf16[1,1,6,128,128]{4,3,2,1,0:T(8,128)(2,1)}, u32[]{:S(2)}) copy-start(bf16[1,1,6,128,128]{4,3,2,1,0:T(8,128)(2,1)} %param.9) | copy-start | bytes 589828
  7.2 154.8 %all-gather.2.cloned.1.call-start = ((), (), s32[]{:S(2)}) async-start(), calls=%async_computation.2 | async-start | bytes 10485760 | tf_op jit(solution)/shard_map/all_gather | solution.py:39
  7.9 6.6 %copy-start.6 = (s32[1,4,6]{2,1,0:T(4,128)S(1)}, s32[1,4,6]{2,1,0:T(4,128)}, u32[]{:S(2)}) copy-start(s32[1,4,6]{2,1,0:T(4,128)} %param.10) | copy-start | bytes 292
  182.0 15.9 %all-to-all-start = ((bf16[1,4,6,128,128]{4,3,2,0,1:T(8,128)(2,1)}), bf16[1,4,6,128,128]{4,3,2,0,1:T(8,128)(2,1)}, u32[]{:S(2)}, u32[]{:S(2)}) async-start(bf16[1,4,6,128,128]{4,3,2,0,1:T(8,128)(2,1)} %bitcast.125), calls=%async_computation | async-start | bytes 1572864 | tf_op jit(solution)/shard_map/all_to_all | solution.py:64
  190.5 2.0 copy-start.8
  198.0 15.1 %all-to-all-start.1 = ((bf16[2,4,3,128,128]{4,3,2,0,1:T(8,128)(2,1)}), bf16[2,4,3,128,128]{4,3,2,0,1:T(8,128)(2,1)S(1)}, u32[]{:S(2)}, u32[]{:S(2)}) async-start(bf16[2,4,3,128,128]{4,3,2,0,1:T(8,128)(2,1)} %copy.77), calls=%async_computation.1 | async-start | bytes 1572864 | tf_op jit(solution)/shard_map/all_to_all | solution.py:65
  201.5 11.7 %copy-start.3 = (bf16[2,128,128]{2,1,0:T(8,128)(2,1)S(1)}, bf16[2,128,128]{2,1,0:T(8,128)(2,1)}, u32[]{:S(2)}) copy-start(bf16[2,128,128]{2,1,0:T(8,128)(2,1)} %param.12) | copy-start | bytes 196612
  201.5 11.7 %copy-start.7 = (pred[2,3]{1,0:T(4,128)(4,1)S(1)}, pred[2,3]{1,0:T(4,128)(4,1)}, u32[]{:S(2)}) copy-start(pred[2,3]{1,0:T(4,128)(4,1)} %get-tuple-element.34) | copy-start | bytes 22
  201.5 41.8 %all-reduce.4.cloned.1.call-start = ((), (), s32[]{:S(2)}) async-start(), calls=%async_computation.3 | async-start | bytes 131072 | tf_op jit(solution)/shard_map/psum | solution.py:89
  203.6 39.6 %copy-start.4 = (f32[2,128,128]{2,1,0:T(8,128)S(1)}, f32[2,128,128]{2,1,0:T(8,128)}, u32[]{:S(2)}) copy-start(f32[2,128,128]{2,1,0:T(8,128)} %param.15) | copy-start | bytes 393220
  203.7 74.4 %copy-start.5 = (f32[1,128,128]{2,1,0:T(8,128)S(1)}, f32[1,128,128]{2,1,0:T(8,128)}, u32[]{:S(2)}) copy-start(f32[1,128,128]{2,1,0:T(8,128)} %param.14) | copy-start | bytes 196612
  213.8 72.1 %copy-start.2 = (bf16[2,3,128,128]{3,2,1,0:T(8,128)(2,1)}, bf16[2,3,128,128]{3,2,1,0:T(8,128)(2,1)S(1)}, u32[]{:S(2)}) copy-start(bf16[2,3,128,128]{3,2,1,0:T(8,128)(2,1)S(1)} %fusion.3) | copy-start | bytes 589828
  214.7 63.4 %all-reduce.6.cloned.1.call-start = ((), (), s32[]{:S(2)}) async-start(), calls=%async_computation.4 | async-start | bytes 393216 | tf_op jit(solution)/shard_map/psum | solution.py:84
Sparse Core Ops, SparseCore 0:
  9.6 152.3 all-gather.1
  214.8 28.3 all-reduce.3
  246.3 31.7 all-reduce.5
where the time goes:
time: 297 us
  waiting for transfers between devices  218 us (73%)
  local copies, waits for them, and re-layouts  28.5 us (10%)
  matrix products  17.7 us (6%)
  between operations  14 us (5%)
  other arithmetic  10.1 us (3%)
  starting transfers between devices  7.82 us (3%)
    all_gather x1, waiting for transfers between devices, on_device(): lax.all_gather(sigma_top, 'row', axis=0, tiled=True)  145 us
    psum x1, waiting for transfers between devices, on_device(): par_total, row_total = lax.psum((par_piece, row_piece), 'col')  33.6 us
    psum x1, waiting for transfers between devices, on_device(): lax.psum(child_piece.astype(jnp.bfloat16), 'col').astype(jnp.float32)  27.4 us
    dot_general x1, matrix products, on_device(): jnp.dot(lax.all_gather(sigma_top, 'row', axis=0, tiled=True), dense_panel...  9.22 us
    all_to_all x1, waiting for transfers between devices, on_device(): lax.all_to_all(child_partial, 'col', split_axis=1, concat_axis=1, tiled=T...  7.76 us
  transfers between devices with their start and end apart: 5, of which 5 were waited for; matrix products, arithmetic and copies ran while one was open for 8% of the time, Pallas kernels for 0%

commit v1 on v0

--- a/solution.py
+++ b/solution.py
@@ -1,6 +1,10 @@
+import functools
+
 import jax
 import jax.numpy as jnp
 from jax import lax
+from jax.experimental import pallas as pl
+from jax.experimental.pallas import tpu as pltpu
 from jax.sharding import PartitionSpec as P
 
 PRECISE = lax.Precision.HIGHEST
@@ -98,6 +102,509 @@
     return (par_column, par_var, child_column, child_row, child_var)
 
 
+ROWS = 4
+COLS = 4
+LANES = 128
+
+
+def transposed_dot(a, b, precision=None):
+    return lax.dot_general(
+        a, b, (((0,), (0,)), ((), ())), preferred_element_type=jnp.float32, precision=precision
+    )
+
+
+def fused_kernel(
+    slots,
+    picks,
+    kids,
+    sig,
+    ppan,
+    cpan,
+    top,
+    lst,
+    pinv,
+    cinv,
+    pcol,
+    pvar,
+    ccol,
+    crow,
+    cvar,
+    pan_all,
+    own_part,
+    sib_part,
+    pair_sum,
+    z_recv,
+    x_recv,
+    list_all,
+    dense,
+    dense_out,
+    tail_recv,
+    in_send,
+    in_recv,
+    lst_send,
+    lst_recv,
+    sib_send,
+    sib_recv,
+    z_send,
+    z_recv_sem,
+    x_send,
+    x_recv_sem,
+    tail_send,
+    tail_recv_sem,
+):
+    width = LANES
+    blocks = slots + kids * picks
+    z = lax.axis_index("row")
+    col = lax.axis_index("col")
+    core = lax.rem(col, 2)
+    xpos = lax.div(col, 2)
+    chip = xpos * 2
+    sibling = chip + 1 - core
+    across = (1 - xpos) * 2 + core
+
+    def remote(src, dst, send, recv, row, column):
+        return pltpu.make_async_remote_copy(
+            src_ref=src,
+            dst_ref=dst,
+            send_sem=send,
+            recv_sem=recv,
+            device_id={"row": row, "col": column},
+            device_id_type=pl.DeviceIdType.MESH,
+        )
+
+    def visit(t):
+        p = jnp.int32(0)
+        for zz in range(ROWS):
+            nearest = sorted(range(ROWS), key=lambda q: (abs(q - zz), (q < zz) == (zz >= 2)))
+            for tt in range(ROWS):
+                p = jnp.where((z == zz) & (t == tt), nearest[tt], p)
+        return p
+
+    barrier = pltpu.get_barrier_semaphore()
+    for step in range(1, ROWS):
+        for k in range(2):
+            pl.semaphore_signal(
+                barrier,
+                inc=1,
+                device_id={"row": lax.rem(z + step, ROWS), "col": chip + k},
+                device_id_type=pl.DeviceIdType.MESH,
+            )
+    pl.semaphore_signal(
+        barrier, inc=1, device_id={"row": z, "col": sibling}, device_id_type=pl.DeviceIdType.MESH
+    )
+    for k in range(2):
+        pl.semaphore_signal(
+            barrier,
+            inc=1,
+            device_id={"row": z, "col": (1 - xpos) * 2 + k},
+            device_id_type=pl.DeviceIdType.MESH,
+        )
+    pl.semaphore_wait(barrier, 2 * ROWS + 1)
+
+    own_parts = (ppan, cpan)
+    bounds = ((0, slots), (slots, kids * picks))
+
+    def list_copy(step):
+        target = lax.rem(z + step, ROWS)
+        return remote(
+            lst.at[0], list_all.at[z], lst_send.at[target], lst_recv.at[z], target, col
+        )
+
+    def list_arrival(p):
+        return remote(lst.at[0], list_all.at[p], lst_send.at[p], lst_recv.at[p], p, col)
+
+    def panel_part(p, part):
+        first, count = bounds[part]
+        return pan_all.at[p, pl.ds(first, count)]
+
+    def own_copy(part, up):
+        return remote(
+            own_parts[part],
+            panel_part(z, part),
+            in_send.at[up, z, part],
+            in_recv.at[z, part],
+            z + 1 if up else z - 1,
+            col,
+        )
+
+    def forward(p, part, up):
+        return remote(
+            panel_part(p, part),
+            panel_part(p, part),
+            in_send.at[up, p, part],
+            in_recv.at[p, part],
+            z + 1 if up else z - 1,
+            col,
+        )
+
+    for step in range(1, ROWS):
+        list_copy(step).start()
+    for part in range(2):
+
+        @pl.when(z < ROWS - 1)
+        def _():
+            own_copy(part, 1).start()
+
+        @pl.when(z > 0)
+        def _():
+            own_copy(part, 0).start()
+
+    for part in range(2):
+        first, count = bounds[part]
+        pan_all[z, pl.ds(first, count)] = own_parts[part][...]
+    list_all[z] = lst[0]
+
+    def sib_copy(p):
+        slot = lax.div(p, 2)
+        return remote(
+            own_part.at[p], sib_part.at[slot], sib_send.at[slot], sib_recv.at[slot], z, sibling
+        )
+
+    def z_copy(p):
+        slot = lax.div(p, 2)
+        here = lax.div(z, 2)
+        return remote(
+            pair_sum.at[slot],
+            z_recv.at[here],
+            z_send.at[slot],
+            z_recv_sem.at[here],
+            p,
+            chip + lax.rem(z, 2),
+        )
+
+    group_blocks = sig.shape[1] // width
+    spans = [(q, group_blocks - slots + q + 1) for q in range(slots)]
+    spans += [
+        (s, group_blocks - picks + s + 1) for _ in range(kids) for s in range(picks)
+    ]
+    panel_of = [0] * slots + [1 + kid for kid in range(kids) for _ in range(picks)]
+
+    def places(table):
+        table = table.astype(jnp.float32)
+        return [jnp.broadcast_to(table[e : e + 1], (width, width)) for e in range(blocks)]
+
+    @pl.loop(0, ROWS + 1)
+    def _(t):
+        @pl.when(t < ROWS)
+        def _():
+            p = visit(t)
+
+            @pl.when(p != z)
+            def _():
+                for part in range(2):
+                    forward(p, part, 0).wait_recv()
+
+                    @pl.when((p < z) & (z < ROWS - 1))
+                    def _():
+                        forward(p, part, 1).start()
+
+                    @pl.when((p > z) & (z > 0))
+                    def _():
+                        forward(p, part, 0).start()
+
+                list_arrival(p).wait_recv()
+
+            at = places(list_all[p, col])
+            for panel in range(1 + kids):
+                entries = [e for e in range(blocks) if panel_of[e] == panel]
+                for b in range(group_blocks):
+                    value = jnp.zeros((width, width), jnp.float32)
+                    for e in entries:
+                        if spans[e][0] <= b < spans[e][1]:
+                            value = jnp.where(at[e] == b, pan_all[p, e].astype(jnp.float32), value)
+                    dense[pl.ds(b * width, width), pl.ds(panel * width, width)] = value.astype(
+                        jnp.bfloat16
+                    )
+            dense_out[...] = jnp.dot(sig[...], dense[...], preferred_element_type=jnp.float32)
+            at = places(list_all[p, z])
+            for e in range(blocks):
+                first, end = spans[e]
+                lane = pl.ds(panel_of[e] * width, width)
+                value = dense_out[pl.ds(first * width, width), lane]
+                for b in range(first + 1, end):
+                    value = jnp.where(
+                        at[e] == b, dense_out[pl.ds(b * width, width), lane], value
+                    )
+                own_part[p, e] = value.astype(jnp.bfloat16)
+
+            @pl.when(lax.rem(p, 2) != core)
+            def _():
+                sib_copy(p).start()
+
+        @pl.when(t > 0)
+        def _():
+            p = visit(t - 1)
+
+            @pl.when(lax.rem(p, 2) == core)
+            def _():
+                slot = lax.div(p, 2)
+                sib_copy(p).wait_recv()
+
+                @pl.loop(0, blocks)
+                def _(b):
+                    total = own_part[p, b].astype(jnp.float32) + sib_part[slot, b].astype(
+                        jnp.float32
+                    )
+                    pair_sum[slot, b] = total.astype(jnp.bfloat16)
+
+                @pl.when(p == z)
+                def _():
+                    z_recv[slot] = pair_sum[slot]
+
+                @pl.when(p != z)
+                def _():
+                    z_copy(p).start()
+
+    precise = lax.Precision.HIGHEST
+    gram = transposed_dot(pinv[...], pinv[...], precise)
+    wide_top = [top[kid].astype(jnp.float32) for kid in range(kids)]
+    gram_top = [
+        jnp.dot(gram, wide, precision=precise, preferred_element_type=jnp.float32)
+        for wide in wide_top
+    ]
+
+    def z_arrival(slot):
+        source = core + 2 * slot
+        return remote(
+            pair_sum.at[slot],
+            z_recv.at[slot],
+            z_send.at[slot],
+            z_recv_sem.at[slot],
+            source,
+            chip + lax.rem(z, 2),
+        )
+
+    x_copy = remote(z_recv.at[1 - xpos], x_recv, x_send, x_recv_sem, z, across)
+
+    @pl.when(core + 2 * (1 - xpos) != z)
+    def _():
+        z_arrival(1 - xpos).wait_recv()
+
+    x_copy.start()
+
+    @pl.when(core + 2 * xpos != z)
+    def _():
+        z_arrival(xpos).wait_recv()
+
+    x_copy.wait_recv()
+
+    own_slots = places(lst[1, col])
+    par_diag = jnp.zeros((1, width), jnp.float32)
+    for q in range(slots):
+        total = z_recv[xpos, q].astype(jnp.float32) + x_recv[q].astype(jnp.float32)
+        column = (-total).astype(jnp.bfloat16)
+        pcol[q] = column
+        par_diag += jnp.sum(
+            ppan[q].astype(jnp.float32) * column.astype(jnp.float32), axis=0, keepdims=True
+        )
+    par_piece = transposed_dot(
+        ppan[...].reshape(slots * width, width), pcol[...].reshape(slots * width, width)
+    )
+    tail_recv[col, pl.ds(kids * width, 8)] = jnp.zeros((8, width), jnp.float32)
+    tail_recv[col, pl.ds(kids * width, 1)] = par_diag
+    for kid in range(kids):
+        kid_diag = jnp.zeros((1, width), jnp.float32)
+        selected = []
+        for s in range(picks):
+            value = pcol[s].astype(jnp.float32)
+            for q in range(s + 1, slots - picks + s + 1):
+                value = jnp.where(
+                    own_slots[slots + kid * picks + s] == q, pcol[q].astype(jnp.float32), value
+                )
+            selected.append(value.astype(jnp.bfloat16))
+        piece = transposed_dot(
+            jnp.concatenate(selected, axis=0),
+            cpan[pl.ds(kid * picks, picks)].reshape(picks * width, width),
+        )
+        piece = piece - jnp.dot(
+            par_piece, wide_top[kid], precision=precise, preferred_element_type=jnp.float32
+        )
+        tail_recv[col, pl.ds(kid * width, width)] = piece
+        for s in range(picks):
+            at = kid * picks + s
+            upper = (
+                z_recv[xpos, slots + at].astype(jnp.float32)
+                + x_recv[slots + at].astype(jnp.float32)
+                + jnp.dot(selected[s], top[kid], preferred_element_type=jnp.float32)
+            )
+            column = (-upper).astype(jnp.bfloat16)
+            ccol[at] = column
+            kid_diag += jnp.sum(
+                cpan[at].astype(jnp.float32) * column.astype(jnp.float32), axis=0, keepdims=True
+            )
+        tail_recv[col, pl.ds(kids * width + 1 + kid, 1)] = kid_diag
+
+    def tail_copy(step):
+        target = lax.rem(col + step, COLS)
+        return remote(
+            tail_recv.at[col],
+            tail_recv.at[col],
+            tail_send.at[target],
+            tail_recv_sem.at[col],
+            z,
+            target,
+        )
+
+    def tail_arrival(source):
+        return remote(
+            tail_recv.at[source],
+            tail_recv.at[source],
+            tail_send.at[source],
+            tail_recv_sem.at[source],
+            z,
+            source,
+        )
+
+    for step in range(1, COLS):
+        tail_copy(step).start()
+    for step in range(1, COLS):
+        tail_arrival(lax.rem(col + step, COLS)).wait_recv()
+    sums = [tail_recv[c, pl.ds(kids * width, 8)] for c in range(COLS)]
+    diags = sums[0] + sums[1] + sums[2] + sums[3]
+    pvar[...] = jnp.sum(pinv[...] * pinv[...], axis=0, keepdims=True) - diags[0:1]
+    for kid in range(kids):
+        part = [tail_recv[c, pl.ds(kid * width, width)] for c in range(COLS)]
+        rows = part[0] + part[1] + part[2] + part[3] + gram_top[kid]
+        crow[kid] = (-rows).astype(jnp.bfloat16)
+        inv = cinv[kid]
+        cvar[pl.ds(kid, 1), :] = (
+            jnp.sum(inv * inv, axis=0, keepdims=True)
+            - diags[1 + kid : 2 + kid]
+            + jnp.sum(wide_top[kid] * rows, axis=0, keepdims=True)
+        )
+
+    for step in range(1, ROWS):
+        list_copy(step).wait_send()
+    for step in range(1, COLS):
+        tail_copy(step).wait_send()
+    for part in range(2):
+
+        @pl.when(z < ROWS - 1)
+        def _():
+            own_copy(part, 1).wait_send()
+
+        @pl.when(z > 0)
+        def _():
+            own_copy(part, 0).wait_send()
+
+        for p in range(ROWS):
+
+            @pl.when((p < z) & (z < ROWS - 1))
+            def _():
+                forward(p, part, 1).wait_send()
+
+            @pl.when((p > z) & (z > 0))
+            def _():
+                forward(p, part, 0).wait_send()
+
+    for slot in range(2):
+        sib_copy(1 - core + 2 * slot).wait_send()
+
+        @pl.when(core + 2 * slot != z)
+        def _():
+            z_copy(core + 2 * slot).wait_send()
+
+    x_copy.wait_send()
+
+
+def fits_kernel(
+    mesh, sigma_top, par_panel, par_list, child_panel, child_top, child_list, par_inv, child_inv
+):
+    groups = par_list.shape[1]
+    order = sigma_top.shape[1]
+    return (
+        mesh.shape["row"] == ROWS
+        and mesh.shape["col"] == COLS
+        and groups == COLS
+        and sigma_top.shape[0] == order
+        and par_panel.shape[0] == 1
+        and par_panel.shape[-1] == LANES
+        and child_panel.shape[0] <= 7
+        and order * order <= 1 << 22
+    )
+
+
+def on_device_kernel(
+    sigma_top, par_panel, par_list, child_panel, child_top, child_list, par_inv, child_inv
+):
+    slots = par_panel.shape[2]
+    kids, _, picks = child_panel.shape[:3]
+    width = LANES
+    blocks = slots + kids * picks
+
+    group_blocks = sigma_top.shape[1] // width
+    par_here = par_list[0]
+    hit = child_list[..., None] == jnp.arange(slots, dtype=jnp.int32)
+    child_place = jnp.sum(jnp.where(hit, par_here[None, :, None, :], 0), axis=-1)
+    pad = -blocks % 16
+
+    def table(children):
+        rows = jnp.moveaxis(children, 0, 1).reshape(COLS, kids * picks)
+        rows = jnp.concatenate([par_here, rows], axis=1)
+        return jnp.pad(rows, ((0, 0), (0, pad)))
+
+    lists = jnp.stack([table(child_place), table(child_list)]).astype(jnp.bfloat16)
+    lists = jnp.broadcast_to(lists[..., None], lists.shape + (LANES,))
+    bf16, f32 = jnp.bfloat16, jnp.float32
+    vmem = pl.BlockSpec(memory_space=pltpu.VMEM)
+    dma = pltpu.SemaphoreType.DMA
+    outs = pl.pallas_call(
+        functools.partial(fused_kernel, slots, picks, kids),
+        out_shape=(
+            jax.ShapeDtypeStruct((slots, width, width), bf16),
+            jax.ShapeDtypeStruct((1, width), f32),
+            jax.ShapeDtypeStruct((kids * picks, width, width), bf16),
+            jax.ShapeDtypeStruct((kids, width, width), bf16),
+            jax.ShapeDtypeStruct((kids, width), f32),
+        ),
+        in_specs=[vmem] * 7,
+        out_specs=[vmem] * 5,
+        scratch_shapes=[
+            pltpu.VMEM((ROWS, blocks, width, width), bf16),
+            pltpu.VMEM((ROWS, blocks, width, width), bf16),
+            pltpu.VMEM((2, blocks, width, width), bf16),
+            pltpu.VMEM((2, blocks, width, width), bf16),
+            pltpu.VMEM((2, blocks, width, width), bf16),
+            pltpu.VMEM((blocks, width, width), bf16),
+            pltpu.VMEM((ROWS, COLS, blocks + pad, LANES), bf16),
+            pltpu.VMEM((group_blocks * width, (1 + kids) * width), bf16),
+            pltpu.VMEM((group_blocks * width, (1 + kids) * width), f32),
+            pltpu.VMEM((COLS, kids * width + 8, width), f32),
+            dma((2, ROWS, 2)),
+            dma((ROWS, 2)),
+            dma((ROWS,)),
+            dma((ROWS,)),
+            dma((2,)),
+            dma((2,)),
+            dma((2,)),
+            dma((2,)),
+            dma,
+            dma,
+            dma((COLS,)),
+            dma((COLS,)),
+        ],
+        compiler_params=pltpu.CompilerParams(
+            collective_id=0, has_side_effects=True, vmem_limit_bytes=40 * 1024 * 1024
+        ),
+    )(
+        sigma_top,
+        par_panel.reshape(slots, width, width),
+        child_panel.reshape(kids * picks, width, width),
+        child_top,
+        lists,
+        par_inv.reshape(width, width),
+        child_inv,
+    )
+    pcol, pvar, ccol, crow, cvar = outs
+    return (
+        pcol.reshape(par_panel.shape),
+        pvar,
+        ccol.reshape(child_panel.shape),
+        crow,
+        cvar,
+    )
+
+
 def solution(mesh):
     in_specs = (
         P(("cfg", "row"), "col"),
@@ -116,6 +623,11 @@
         P(("cfg", "row"), None, None),
         P(("cfg", "row"), None),
     )
+    def body(*args):
+        if fits_kernel(mesh, *args):
+            return on_device_kernel(*args)
+        return on_device(*args)
+
     return jax.shard_map(
-        on_device, mesh=mesh, in_specs=in_specs, out_specs=out_specs, check_vma=False
-    )
+        body, mesh=mesh, in_specs=in_specs, out_specs=out_specs, check_vma=False
+    )

time: 297 us -> 83.5 us (0.28)
  waiting for transfers between devices: 218 us -> 0 us
  Pallas kernels: 0 us -> 69.1 us
  local copies, waits for them, and re-layouts: 28.5 us -> 10.2 us
  matrix products: 17.7 us -> 0 us
  between operations: 14 us -> 0.68 us
  starting transfers between devices: 7.82 us -> 0 us
  other arithmetic: 10.1 us -> 2.4 us
    all_gather x1 -> x0, waiting for transfers between devices: 145 us -> none  [on_device(): lax.all_gather(sigma_top, 'row', axis=0, tiled=True)]
    pallas_call x0 -> x1, Pallas kernels: none -> 69.1 us  [on_device_kernel(): pl.pallas_call(functools.partial(fused_kernel, slots, picks, kids), out_s...]
    psum x2 -> x0, waiting for transfers between devices: 61 us -> none  [the longest x1 33.6 us: on_device(): par_total, row_total = lax.psum((par_piece, row_piece), 'col')]
    dot_general x11 -> x0, matrix products: 17.7 us -> none  [the longest x1 9.22 us: on_device(): jnp.dot(lax.all_gather(sigma_top, 'row', axis=0, tiled=True), dense_panel...]
    gather x18 -> x0, local copies, waits for them, and re-layouts: 11.9 us -> none  [the longest x2 4.7 us: pick_blocks(): found_rows = jnp.take(product_blocks, block_index.reshape(-1), axis=0)]
    all_to_all x2 -> x0, waiting for transfers between devices: 11.6 us -> none  [the longest x1 7.76 us: on_device(): lax.all_to_all(child_partial, 'col', split_axis=1, concat_axis=1, tiled=T...]
    all_to_all x2 -> x0, starting transfers between devices: 7.7 us -> none  [the longest x1 4.21 us: on_device(): lax.all_to_all(par_partial, 'col', split_axis=1, concat_axis=1, tiled=True)]
    unnamed x21 -> x18, local copies, waits for them, and re-layouts: 3.98 us -> 9.76 us
  transfers between devices with their start and end apart: 5 -> 0, of which waited for: 5 -> 0; matrix products, arithmetic and copies ran while one was open for 8% -> 0% of each run, Pallas kernels for 0% -> 0%
where the time goes in v1:
time: 83.5 us; the launch traced here: 82.3 us
  Pallas kernels  69.1 us (83%)
  local copies, waits for them, and re-layouts  10.2 us (12%)
  other arithmetic  2.4 us (3%)
    pallas_call x1, Pallas kernels, on_device_kernel(): pl.pallas_call(functools.partial(fused_kernel, slots, picks, kids), out_s...  69.1 us
    unnamed x18, local copies, waits for them, and re-layouts  9.76 us

profile of v1, /device:TPU:0, one launch (start us, length us, event | category | flops | bytes accessed | tf_op | source)
XLA Modules:
  0.0 82.3 jit_solution(4595538783245540823)
XLA Ops:
  0.6 0.7 bitcast_convert_fusion
  1.3 0.7 convert_bitcast_fusion.1
  2.0 0.1 copy.21
  2.1 0.1 reshape.57
  2.2 0.7 copy.19
  2.9 0.9 %select_reduce_fusion = s32[2,4,3]{1,2,0:T(4,128)S(1)} fusion(s32[4,6]{1,0:T(4,128)} %bitcast.24, s32[2,4,3]{1,2,0:T(4,128)S(1)} %copy.19), kind=kLoop, calls=%fused_computation | loop fusion | flops 408 | bytes 288 | tf_op jit(solution)/shard_map/reduce_sum | solution.py:538
  3.8 0.1 copy.23
  4.0 0.1 pad_maximum_fusion.1
  4.1 0.1 broadcast_in_dim.22.lst
  4.2 0.0 copy-start
  4.2 1.6 %copy-done = bf16[1024,1024]{1,0:T(8,128)(2,1)S(1)} copy-done((bf16[1024,1024]{1,0:T(8,128)(2,1)S(1)}, bf16[1024,1024]{1,0:T(8,128)(2,1)}, u32[]{:S(2)}) %copy-start) | copy-done | bytes 2097176
  5.8 0.0 copy-start.1
  5.8 0.9 %copy-done.1 = bf16[1,1,6,128,128]{4,3,2,1,0:T(8,128)(2,1)S(1)} copy-done((bf16[1,1,6,128,128]{4,3,2,1,0:T(8,128)(2,1)S(1)}, bf16[1,1,6,128,128]{4,3,2,1,0:T(8,128)(2,1)}, u32[]{:S(2)}) %copy-start.1) | copy-done | bytes 196632
  6.7 0.0 copy-start.2
  6.7 0.9 %copy-done.2 = bf16[2,1,3,128,128]{4,3,2,1,0:T(8,128)(2,1)S(1)} copy-done((bf16[2,1,3,128,128]{4,3,2,1,0:T(8,128)(2,1)S(1)}, bf16[2,1,3,128,128]{4,3,2,1,0:T(8,128)(2,1)}, u32[]{:S(2)}) %copy-start.2) | copy-done | bytes 196632
  7.6 0.0 copy-start.3
  7.6 0.9 %copy-done.3 = f32[2,128,128]{2,1,0:T(8,128)S(1)} copy-done((f32[2,128,128]{2,1,0:T(8,128)S(1)}, f32[2,128,128]{2,1,0:T(8,128)}, u32[]{:S(2)}) %copy-start.3) | copy-done | bytes 131096
  8.5 0.0 copy-start.4
  8.5 0.8 %copy-done.4 = bf16[2,128,128]{2,1,0:T(8,128)(2,1)S(1)} copy-done((bf16[2,128,128]{2,1,0:T(8,128)(2,1)S(1)}, bf16[2,128,128]{2,1,0:T(8,128)(2,1)}, u32[]{:S(2)}) %copy-start.4) | copy-done | bytes 65560
  9.4 0.0 copy-start.5
  9.4 0.8 %copy-done.5 = f32[1,128,128]{2,1,0:T(8,128)S(1)} copy-done((f32[1,128,128]{2,1,0:T(8,128)S(1)}, f32[1,128,128]{2,1,0:T(8,128)}, u32[]{:S(2)}) %copy-start.5) | copy-done | bytes 65560
  10.2 69.1 %shard_map.119 = (bf16[6,128,128]{2,1,0:T(8,128)(2,1)S(1)}, f32[1,128]{1,0:T(1,128)S(1)}, bf16[6,128,128]{2,1,0:T(8,128)(2,1)S(1)}, bf16[2,128,128]{2,1,0:T(8,128)(2,1)S(1)}, f32[2,128]{1,0:T(2,128)S(1)}) custom-call(bf16[1024,1024]{1,0:T(8,128)(2,1)S(1)} %copy-done, bf16[6,128,128]{2,1,0:T(8,128)(2,1)S(1)} %bitcast.21, bf16[6,128,128]{2,1,0:T(8,128)(2,1)S(1)} %bitcast.22, ...), custom_call_target="tpu_custom_call" | custom-call | tf_op jit(solution)/shard_map/pallas_call | solution.py:551
  79.3 0.7 copy.29
  79.9 0.5 copy.30
  80.4 0.7 copy.31
  81.1 0.6 copy.32
  81.7 0.6 copy.33
  (4 shorter events, 0.0 us)
Async XLA Ops:
  4.2 1.6 %copy-start = (bf16[1024,1024]{1,0:T(8,128)(2,1)S(1)}, bf16[1024,1024]{1,0:T(8,128)(2,1)}, u32[]{:S(2)}) copy-start(bf16[1024,1024]{1,0:T(8,128)(2,1)} %sig.1) | copy-start | bytes 6291460
  5.8 0.9 %copy-start.1 = (bf16[1,1,6,128,128]{4,3,2,1,0:T(8,128)(2,1)S(1)}, bf16[1,1,6,128,128]{4,3,2,1,0:T(8,128)(2,1)}, u32[]{:S(2)}) copy-start(bf16[1,1,6,128,128]{4,3,2,1,0:T(8,128)(2,1)} %param.9) | copy-start | bytes 589828
  6.7 0.9 %copy-start.2 = (bf16[2,1,3,128,128]{4,3,2,1,0:T(8,128)(2,1)S(1)}, bf16[2,1,3,128,128]{4,3,2,1,0:T(8,128)(2,1)}, u32[]{:S(2)}) copy-start(bf16[2,1,3,128,128]{4,3,2,1,0:T(8,128)(2,1)} %param.11) | copy-start | bytes 589828
  7.6 0.9 %copy-start.3 = (f32[2,128,128]{2,1,0:T(8,128)S(1)}, f32[2,128,128]{2,1,0:T(8,128)}, u32[]{:S(2)}) copy-start(f32[2,128,128]{2,1,0:T(8,128)} %cinv.1) | copy-start | bytes 393220
  8.5 0.8 %copy-start.4 = (bf16[2,128,128]{2,1,0:T(8,128)(2,1)S(1)}, bf16[2,128,128]{2,1,0:T(8,128)(2,1)}, u32[]{:S(2)}) copy-start(bf16[2,128,128]{2,1,0:T(8,128)(2,1)} %top.1) | copy-start | bytes 196612
  9.4 0.8 %copy-start.5 = (f32[1,128,128]{2,1,0:T(8,128)S(1)}, f32[1,128,128]{2,1,0:T(8,128)}, u32[]{:S(2)}) copy-start(f32[1,128,128]{2,1,0:T(8,128)} %param.14) | copy-start | bytes 196612

commit v2 on v1

--- a/solution.py
+++ b/solution.py
@@ -117,13 +117,14 @@
     slots,
     picks,
     kids,
-    sig,
-    ppan,
-    cpan,
-    top,
-    lst,
-    pinv,
-    cinv,
+    sig_hbm,
+    ppan_hbm,
+    cpan_hbm,
+    top_hbm,
+    pinv_hbm,
+    cinv_hbm,
+    par_s,
+    child_s,
     pcol,
     pvar,
     ccol,
@@ -139,6 +140,13 @@
     dense,
     dense_out,
     tail_recv,
+    kid_recv,
+    sig,
+    top,
+    pinv,
+    cinv,
+    table,
+    local_sem,
     in_send,
     in_recv,
     lst_send,
@@ -151,6 +159,8 @@
     x_recv_sem,
     tail_send,
     tail_recv_sem,
+    kid_send,
+    kid_recv_sem,
 ):
     width = LANES
     blocks = slots + kids * picks
@@ -179,6 +189,28 @@
             for tt in range(ROWS):
                 p = jnp.where((z == zz) & (t == tt), nearest[tt], p)
         return p
+
+    bounds = ((0, slots), (slots, kids * picks))
+
+    def panel_part(p, part):
+        first, count = bounds[part]
+        return pan_all.at[p, pl.ds(first, count)]
+
+    loads = [
+        pltpu.make_async_copy(src, dst, local_sem.at[i])
+        for i, (src, dst) in enumerate(
+            (
+                (ppan_hbm, panel_part(z, 0)),
+                (cpan_hbm, panel_part(z, 1)),
+                (sig_hbm, sig),
+                (top_hbm, top),
+                (pinv_hbm, pinv),
+                (cinv_hbm, cinv),
+            )
+        )
+    ]
+    for load in loads:
+        load.start()
 
     barrier = pltpu.get_barrier_semaphore()
     for step in range(1, ROWS):
@@ -199,33 +231,32 @@
             device_id={"row": z, "col": (1 - xpos) * 2 + k},
             device_id_type=pl.DeviceIdType.MESH,
         )
+    table[...] = jnp.zeros_like(table)
+    for g in range(COLS):
+        for q in range(slots):
+            value = par_s[0, g, q].astype(jnp.float32)
+            table[g, pl.ds(q, 1), :] = jnp.full((1, width), value, jnp.float32)
+        for kid in range(kids):
+            for pick in range(picks):
+                slot = child_s[kid, g, pick]
+                place = par_s[0, g, pick]
+                for q in range(pick + 1, slots - picks + pick + 1):
+                    place = jnp.where(slot == q, par_s[0, g, q], place)
+                value = place.astype(jnp.float32)
+                table[g, pl.ds(slots + kid * picks + pick, 1), :] = jnp.full(
+                    (1, width), value, jnp.float32
+                )
+    list_all[z] = table[...].astype(jnp.bfloat16)
     pl.semaphore_wait(barrier, 2 * ROWS + 1)
-
-    own_parts = (ppan, cpan)
-    bounds = ((0, slots), (slots, kids * picks))
 
     def list_copy(step):
         target = lax.rem(z + step, ROWS)
         return remote(
-            lst.at[0], list_all.at[z], lst_send.at[target], lst_recv.at[z], target, col
+            list_all.at[z], list_all.at[z], lst_send.at[target], lst_recv.at[z], target, col
         )
 
     def list_arrival(p):
-        return remote(lst.at[0], list_all.at[p], lst_send.at[p], lst_recv.at[p], p, col)
-
-    def panel_part(p, part):
-        first, count = bounds[part]
-        return pan_all.at[p, pl.ds(first, count)]
-
-    def own_copy(part, up):
-        return remote(
-            own_parts[part],
-            panel_part(z, part),
-            in_send.at[up, z, part],
-            in_recv.at[z, part],
-            z + 1 if up else z - 1,
-            col,
-        )
+        return remote(list_all.at[p], list_all.at[p], lst_send.at[p], lst_recv.at[p], p, col)
 
     def forward(p, part, up):
         return remote(
@@ -237,40 +268,83 @@
             col,
         )
 
+    def send_own(part):
+        @pl.when(z < ROWS - 1)
+        def _():
+            forward(z, part, 1).start()
+
+        @pl.when(z > 0)
+        def _():
+            forward(z, part, 0).start()
+
     for step in range(1, ROWS):
         list_copy(step).start()
-    for part in range(2):
-
-        @pl.when(z < ROWS - 1)
-        def _():
-            own_copy(part, 1).start()
-
-        @pl.when(z > 0)
-        def _():
-            own_copy(part, 0).start()
-
-    for part in range(2):
+    loads[0].wait()
+    send_own(0)
+    for load in loads[1:]:
+        load.wait()
+
+    def cut(ref, index, part):
         first, count = bounds[part]
-        pan_all[z, pl.ds(first, count)] = own_parts[part][...]
-    list_all[z] = lst[0]
-
-    def sib_copy(p):
+        return ref.at[index, pl.ds(first, count)]
+
+    def sib_copy(p, part):
         slot = lax.div(p, 2)
         return remote(
-            own_part.at[p], sib_part.at[slot], sib_send.at[slot], sib_recv.at[slot], z, sibling
-        )
-
-    def z_copy(p):
+            cut(own_part, p, part),
+            cut(sib_part, slot, part),
+            sib_send.at[slot, part],
+            sib_recv.at[slot, part],
+            z,
+            sibling,
+        )
+
+    def z_copy(p, part):
         slot = lax.div(p, 2)
         here = lax.div(z, 2)
         return remote(
-            pair_sum.at[slot],
-            z_recv.at[here],
-            z_send.at[slot],
-            z_recv_sem.at[here],
+            cut(pair_sum, slot, part),
+            cut(z_recv, here, part),
+            z_send.at[slot, part],
+            z_recv_sem.at[here, part],
             p,
             chip + lax.rem(z, 2),
         )
+
+    def z_arrival(slot, part):
+        return remote(
+            cut(pair_sum, slot, part),
+            cut(z_recv, slot, part),
+            z_send.at[slot, part],
+            z_recv_sem.at[slot, part],
+            core + 2 * slot,
+            chip + lax.rem(z, 2),
+        )
+
+    def x_copy(part):
+        first, count = bounds[part]
+        return remote(
+            cut(z_recv, 1 - xpos, part),
+            x_recv.at[pl.ds(first, count)],
+            x_send.at[part],
+            x_recv_sem.at[part],
+            z,
+            across,
+        )
+
+    def send_across(part):
+        @pl.when(core + 2 * (1 - xpos) != z)
+        def _():
+            z_arrival(1 - xpos, part).wait_recv()
+
+        x_copy(part).start()
+
+    def take_across(part):
+        @pl.when(core + 2 * xpos != z)
+        def _():
+            z_arrival(xpos, part).wait_recv()
+
+        x_copy(part).wait_recv()
 
     group_blocks = sig.shape[1] // width
     spans = [(q, group_blocks - slots + q + 1) for q in range(slots)]
@@ -279,19 +353,66 @@
     ]
     panel_of = [0] * slots + [1 + kid for kid in range(kids) for _ in range(picks)]
 
-    def places(table):
-        table = table.astype(jnp.float32)
-        return [jnp.broadcast_to(table[e : e + 1], (width, width)) for e in range(blocks)]
-
-    @pl.loop(0, ROWS + 1)
-    def _(t):
-        @pl.when(t < ROWS)
+    def places(rows):
+        rows = rows.astype(jnp.float32)
+        return [jnp.broadcast_to(rows[e : e + 1], (width, width)) for e in range(blocks)]
+
+    def compute(p, part):
+        first_entry, count = bounds[part]
+        mine = range(first_entry, first_entry + count)
+        panels = sorted({panel_of[e] for e in mine})
+        low, span = panels[0], len(panels)
+        at = places(list_all[p, col])
+        for panel in panels:
+            entries = [e for e in mine if panel_of[e] == panel]
+            for b in range(group_blocks):
+                value = jnp.zeros((width, width), jnp.float32)
+                for e in entries:
+                    if spans[e][0] <= b < spans[e][1]:
+                        value = jnp.where(at[e] == b, pan_all[p, e].astype(jnp.float32), value)
+                dense[pl.ds(b * width, width), pl.ds(panel * width, width)] = value.astype(
+                    jnp.bfloat16
+                )
+        lanes = pl.ds(low * width, span * width)
+        dense_out[:, lanes] = jnp.dot(
+            sig[...], dense[:, lanes], preferred_element_type=jnp.float32
+        )
+        at = places(list_all[p, z])
+        for e in mine:
+            first, end = spans[e]
+            lane = pl.ds(panel_of[e] * width, width)
+            value = dense_out[pl.ds(first * width, width), lane]
+            for b in range(first + 1, end):
+                value = jnp.where(at[e] == b, dense_out[pl.ds(b * width, width), lane], value)
+            own_part[p, e] = value.astype(jnp.bfloat16)
+
+    def combine(p, part):
+        first, count = bounds[part]
+        slot = lax.div(p, 2)
+        sib_copy(p, part).wait_recv()
+
+        @pl.loop(first, first + count)
+        def _(b):
+            total = own_part[p, b].astype(jnp.float32) + sib_part[slot, b].astype(jnp.float32)
+            pair_sum[slot, b] = total.astype(jnp.bfloat16)
+
+        @pl.when(p == z)
         def _():
-            p = visit(t)
-
-            @pl.when(p != z)
+            z_recv[slot, pl.ds(first, count)] = pair_sum[slot, pl.ds(first, count)]
+
+        @pl.when(p != z)
+        def _():
+            z_copy(p, part).start()
+
+    def stage(part):
+        @pl.loop(0, ROWS + 1)
+        def _(t):
+            @pl.when(t < ROWS)
             def _():
-                for part in range(2):
+                p = visit(t)
+
+                @pl.when(p != z)
+                def _():
                     forward(p, part, 0).wait_recv()
 
                     @pl.when((p < z) & (z < ROWS - 1))
@@ -302,58 +423,37 @@
                     def _():
                         forward(p, part, 0).start()
 
-                list_arrival(p).wait_recv()
-
-            at = places(list_all[p, col])
-            for panel in range(1 + kids):
-                entries = [e for e in range(blocks) if panel_of[e] == panel]
-                for b in range(group_blocks):
-                    value = jnp.zeros((width, width), jnp.float32)
-                    for e in entries:
-                        if spans[e][0] <= b < spans[e][1]:
-                            value = jnp.where(at[e] == b, pan_all[p, e].astype(jnp.float32), value)
-                    dense[pl.ds(b * width, width), pl.ds(panel * width, width)] = value.astype(
-                        jnp.bfloat16
-                    )
-            dense_out[...] = jnp.dot(sig[...], dense[...], preferred_element_type=jnp.float32)
-            at = places(list_all[p, z])
-            for e in range(blocks):
-                first, end = spans[e]
-                lane = pl.ds(panel_of[e] * width, width)
-                value = dense_out[pl.ds(first * width, width), lane]
-                for b in range(first + 1, end):
-                    value = jnp.where(
-                        at[e] == b, dense_out[pl.ds(b * width, width), lane], value
-                    )
-                own_part[p, e] = value.astype(jnp.bfloat16)
-
-            @pl.when(lax.rem(p, 2) != core)
+                    if part == 0:
+                        list_arrival(p).wait_recv()
+
+                if part == 0:
+
+                    @pl.when(t == 1)
+                    def _():
+                        send_own(1)
+
+                compute(p, part)
+
+                @pl.when(lax.rem(p, 2) != core)
+                def _():
+                    sib_copy(p, part).start()
+
+            if part == 1:
+
+                @pl.when(t == ROWS)
+                def _():
+                    send_across(0)
+
+            @pl.when(t > 0)
             def _():
-                sib_copy(p).start()
-
-        @pl.when(t > 0)
-        def _():
-            p = visit(t - 1)
-
-            @pl.when(lax.rem(p, 2) == core)
-            def _():
-                slot = lax.div(p, 2)
-                sib_copy(p).wait_recv()
-
-                @pl.loop(0, blocks)
-                def _(b):
-                    total = own_part[p, b].astype(jnp.float32) + sib_part[slot, b].astype(
-                        jnp.float32
-                    )
-                    pair_sum[slot, b] = total.astype(jnp.bfloat16)
-
-                @pl.when(p == z)
+                p = visit(t - 1)
+
+                @pl.when(lax.rem(p, 2) == core)
                 def _():
-                    z_recv[slot] = pair_sum[slot]
-
-                @pl.when(p != z)
-                def _():
-                    z_copy(p).start()
+                    combine(p, part)
+
+    stage(0)
+    stage(1)
 
     precise = lax.Precision.HIGHEST
     gram = transposed_dot(pinv[...], pinv[...], precise)
@@ -363,148 +463,124 @@
         for wide in wide_top
     ]
 
-    def z_arrival(slot):
-        source = core + 2 * slot
+    def spread(buffer, send, recv, source, target):
         return remote(
-            pair_sum.at[slot],
-            z_recv.at[slot],
-            z_send.at[slot],
-            z_recv_sem.at[slot],
-            source,
-            chip + lax.rem(z, 2),
-        )
-
-    x_copy = remote(z_recv.at[1 - xpos], x_recv, x_send, x_recv_sem, z, across)
-
-    @pl.when(core + 2 * (1 - xpos) != z)
-    def _():
-        z_arrival(1 - xpos).wait_recv()
-
-    x_copy.start()
-
-    @pl.when(core + 2 * xpos != z)
-    def _():
-        z_arrival(xpos).wait_recv()
-
-    x_copy.wait_recv()
-
-    own_slots = places(lst[1, col])
+            buffer.at[source], buffer.at[source], send.at[target], recv.at[source], z, target
+        )
+
+    def send_to_columns(buffer, send, recv):
+        for step in range(1, COLS):
+            spread(buffer, send, recv, col, lax.rem(col + step, COLS)).start()
+
+    def take_from_columns(buffer, send, recv):
+        for step in range(1, COLS):
+            source = lax.rem(col + step, COLS)
+            spread(buffer, send, recv, source, source).wait_recv()
+
+    take_across(0)
     par_diag = jnp.zeros((1, width), jnp.float32)
     for q in range(slots):
         total = z_recv[xpos, q].astype(jnp.float32) + x_recv[q].astype(jnp.float32)
         column = (-total).astype(jnp.bfloat16)
         pcol[q] = column
         par_diag += jnp.sum(
-            ppan[q].astype(jnp.float32) * column.astype(jnp.float32), axis=0, keepdims=True
+            pan_all[z, q].astype(jnp.float32) * column.astype(jnp.float32), axis=0, keepdims=True
         )
     par_piece = transposed_dot(
-        ppan[...].reshape(slots * width, width), pcol[...].reshape(slots * width, width)
-    )
-    tail_recv[col, pl.ds(kids * width, 8)] = jnp.zeros((8, width), jnp.float32)
-    tail_recv[col, pl.ds(kids * width, 1)] = par_diag
+        pan_all[z, pl.ds(0, slots)].reshape(slots * width, width),
+        pcol[...].reshape(slots * width, width),
+    )
+    tail_recv[col, pl.ds(kids * width, 8)] = jnp.broadcast_to(par_diag, (8, width))
+    lifted = []
+    for kid in range(kids):
+        selected = []
+        for s in range(picks):
+            slot = jnp.full((width, width), child_s[kid, col, s], jnp.int32)
+            value = pcol[s].astype(jnp.float32)
+            for q in range(s + 1, slots - picks + s + 1):
+                value = jnp.where(slot == q, pcol[q].astype(jnp.float32), value)
+            selected.append(value.astype(jnp.bfloat16))
+        chosen = jnp.concatenate(selected, axis=0)
+        piece = transposed_dot(
+            chosen,
+            pan_all[z, pl.ds(slots + kid * picks, picks)].reshape(picks * width, width),
+        )
+        piece = piece - jnp.dot(
+            par_piece, wide_top[kid], precision=precise, preferred_element_type=jnp.float32
+        )
+        tail_recv[col, pl.ds(kid * width, width)] = piece
+        lifted.append(jnp.dot(chosen, top[kid], preferred_element_type=jnp.float32))
+    send_across(1)
+    send_to_columns(tail_recv, tail_send, tail_recv_sem)
+
+    take_across(1)
+    kid_diags = []
     for kid in range(kids):
         kid_diag = jnp.zeros((1, width), jnp.float32)
-        selected = []
-        for s in range(picks):
-            value = pcol[s].astype(jnp.float32)
-            for q in range(s + 1, slots - picks + s + 1):
-                value = jnp.where(
-                    own_slots[slots + kid * picks + s] == q, pcol[q].astype(jnp.float32), value
-                )
-            selected.append(value.astype(jnp.bfloat16))
-        piece = transposed_dot(
-            jnp.concatenate(selected, axis=0),
-            cpan[pl.ds(kid * picks, picks)].reshape(picks * width, width),
-        )
-        piece = piece - jnp.dot(
-            par_piece, wide_top[kid], precision=precise, preferred_element_type=jnp.float32
-        )
-        tail_recv[col, pl.ds(kid * width, width)] = piece
         for s in range(picks):
             at = kid * picks + s
             upper = (
                 z_recv[xpos, slots + at].astype(jnp.float32)
                 + x_recv[slots + at].astype(jnp.float32)
-                + jnp.dot(selected[s], top[kid], preferred_element_type=jnp.float32)
+                + lifted[kid][s * width : (s + 1) * width]
             )
             column = (-upper).astype(jnp.bfloat16)
             ccol[at] = column
             kid_diag += jnp.sum(
-                cpan[at].astype(jnp.float32) * column.astype(jnp.float32), axis=0, keepdims=True
+                pan_all[z, slots + at].astype(jnp.float32) * column.astype(jnp.float32),
+                axis=0,
+                keepdims=True,
             )
-        tail_recv[col, pl.ds(kids * width + 1 + kid, 1)] = kid_diag
-
-    def tail_copy(step):
-        target = lax.rem(col + step, COLS)
-        return remote(
-            tail_recv.at[col],
-            tail_recv.at[col],
-            tail_send.at[target],
-            tail_recv_sem.at[col],
-            z,
-            target,
-        )
-
-    def tail_arrival(source):
-        return remote(
-            tail_recv.at[source],
-            tail_recv.at[source],
-            tail_send.at[source],
-            tail_recv_sem.at[source],
-            z,
-            source,
-        )
-
-    for step in range(1, COLS):
-        tail_copy(step).start()
-    for step in range(1, COLS):
-        tail_arrival(lax.rem(col + step, COLS)).wait_recv()
-    sums = [tail_recv[c, pl.ds(kids * width, 8)] for c in range(COLS)]
-    diags = sums[0] + sums[1] + sums[2] + sums[3]
-    pvar[...] = jnp.sum(pinv[...] * pinv[...], axis=0, keepdims=True) - diags[0:1]
+        kid_diags.append(kid_diag)
+    kid_diags.append(jnp.zeros((8 - kids, width), jnp.float32))
+    kid_recv[col] = jnp.concatenate(kid_diags, axis=0)
+    send_to_columns(kid_recv, kid_send, kid_recv_sem)
+
+    take_from_columns(tail_recv, tail_send, tail_recv_sem)
+    par_total = [tail_recv[c, pl.ds(kids * width, 8)][0:1] for c in range(COLS)]
+    pvar[...] = jnp.sum(pinv[...] * pinv[...], axis=0, keepdims=True) - (
+        par_total[0] + par_total[1] + par_total[2] + par_total[3]
+    )
+    known = []
     for kid in range(kids):
         part = [tail_recv[c, pl.ds(kid * width, width)] for c in range(COLS)]
         rows = part[0] + part[1] + part[2] + part[3] + gram_top[kid]
         crow[kid] = (-rows).astype(jnp.bfloat16)
         inv = cinv[kid]
-        cvar[pl.ds(kid, 1), :] = (
+        known.append(
             jnp.sum(inv * inv, axis=0, keepdims=True)
-            - diags[1 + kid : 2 + kid]
             + jnp.sum(wide_top[kid] * rows, axis=0, keepdims=True)
         )
+    take_from_columns(kid_recv, kid_send, kid_recv_sem)
+    kid_total = kid_recv[0] + kid_recv[1] + kid_recv[2] + kid_recv[3]
+    for kid in range(kids):
+        cvar[pl.ds(kid, 1), :] = known[kid] - kid_total[kid : kid + 1]
 
     for step in range(1, ROWS):
         list_copy(step).wait_send()
     for step in range(1, COLS):
-        tail_copy(step).wait_send()
+        target = lax.rem(col + step, COLS)
+        spread(tail_recv, tail_send, tail_recv_sem, col, target).wait_send()
+        spread(kid_recv, kid_send, kid_recv_sem, col, target).wait_send()
     for part in range(2):
-
-        @pl.when(z < ROWS - 1)
-        def _():
-            own_copy(part, 1).wait_send()
-
-        @pl.when(z > 0)
-        def _():
-            own_copy(part, 0).wait_send()
-
         for p in range(ROWS):
 
-            @pl.when((p < z) & (z < ROWS - 1))
+            @pl.when((p <= z) & (z < ROWS - 1))
             def _():
                 forward(p, part, 1).wait_send()
 
-            @pl.when((p > z) & (z > 0))
+            @pl.when((p >= z) & (z > 0))
             def _():
                 forward(p, part, 0).wait_send()
 
-    for slot in range(2):
-        sib_copy(1 - core + 2 * slot).wait_send()
-
-        @pl.when(core + 2 * slot != z)
-        def _():
-            z_copy(core + 2 * slot).wait_send()
-
-    x_copy.wait_send()
+        for slot in range(2):
+            sib_copy(1 - core + 2 * slot, part).wait_send()
+
+            @pl.when(core + 2 * slot != z)
+            def _():
+                z_copy(core + 2 * slot, part).wait_send()
+
+        x_copy(part).wait_send()
 
 
 def fits_kernel(
@@ -533,20 +609,11 @@
     blocks = slots + kids * picks
 
     group_blocks = sigma_top.shape[1] // width
-    par_here = par_list[0]
-    hit = child_list[..., None] == jnp.arange(slots, dtype=jnp.int32)
-    child_place = jnp.sum(jnp.where(hit, par_here[None, :, None, :], 0), axis=-1)
     pad = -blocks % 16
-
-    def table(children):
-        rows = jnp.moveaxis(children, 0, 1).reshape(COLS, kids * picks)
-        rows = jnp.concatenate([par_here, rows], axis=1)
-        return jnp.pad(rows, ((0, 0), (0, pad)))
-
-    lists = jnp.stack([table(child_place), table(child_list)]).astype(jnp.bfloat16)
-    lists = jnp.broadcast_to(lists[..., None], lists.shape + (LANES,))
     bf16, f32 = jnp.bfloat16, jnp.float32
     vmem = pl.BlockSpec(memory_space=pltpu.VMEM)
+    smem = pl.BlockSpec(memory_space=pltpu.SMEM)
+    hbm = pl.BlockSpec(memory_space=pltpu.HBM)
     dma = pltpu.SemaphoreType.DMA
     outs = pl.pallas_call(
         functools.partial(fused_kernel, slots, picks, kids),
@@ -557,7 +624,7 @@
             jax.ShapeDtypeStruct((kids, width, width), bf16),
             jax.ShapeDtypeStruct((kids, width), f32),
         ),
-        in_specs=[vmem] * 7,
+        in_specs=[hbm] * 6 + [smem] * 2,
         out_specs=[vmem] * 5,
         scratch_shapes=[
             pltpu.VMEM((ROWS, blocks, width, width), bf16),
@@ -570,16 +637,25 @@
             pltpu.VMEM((group_blocks * width, (1 + kids) * width), bf16),
             pltpu.VMEM((group_blocks * width, (1 + kids) * width), f32),
             pltpu.VMEM((COLS, kids * width + 8, width), f32),
+            pltpu.VMEM((COLS, 8, width), f32),
+            pltpu.VMEM(sigma_top.shape, bf16),
+            pltpu.VMEM(child_top.shape, bf16),
+            pltpu.VMEM((width, width), f32),
+            pltpu.VMEM(child_inv.shape, f32),
+            pltpu.VMEM((COLS, blocks + pad, LANES), f32),
+            dma((6,)),
             dma((2, ROWS, 2)),
             dma((ROWS, 2)),
             dma((ROWS,)),
             dma((ROWS,)),
+            dma((2, 2)),
+            dma((2, 2)),
+            dma((2, 2)),
+            dma((2, 2)),
             dma((2,)),
             dma((2,)),
-            dma((2,)),
-            dma((2,)),
-            dma,
-            dma,
+            dma((COLS,)),
+            dma((COLS,)),
             dma((COLS,)),
             dma((COLS,)),
         ],
@@ -591,9 +667,10 @@
         par_panel.reshape(slots, width, width),
         child_panel.reshape(kids * picks, width, width),
         child_top,
-        lists,
         par_inv.reshape(width, width),
         child_inv,
+        par_list,
+        child_list,
     )
     pcol, pvar, ccol, crow, cvar = outs
     return (

time: 83.5 us -> 75.2 us (0.901)
  Pallas kernels: 69.1 us -> 63 us
  other arithmetic: 2.4 us -> 0 us
    pallas_call x1, Pallas kernels: 69.1 us -> 63 us  [on_device_kernel(): pl.pallas_call(functools.partial(fused_kernel, slots, picks, kids), out_s...]
    reduce_sum x1 -> x0, other arithmetic: 0.92 us -> none  [on_device_kernel(): jnp.sum(jnp.where(hit, par_here[None, :, None, :], 0), axis=-1)]
    unnamed x18 -> x20, local copies, waits for them, and re-layouts: 9.76 us -> 10.5 us
where the time goes in v2:
time: 75.2 us; the launch traced here: 74.2 us
  Pallas kernels  63 us (84%)
  local copies, waits for them, and re-layouts  10.5 us (14%)
    pallas_call x1, Pallas kernels, on_device_kernel(): pl.pallas_call(functools.partial(fused_kernel, slots, picks, kids), out_s...  63 us
    unnamed x20, local copies, waits for them, and re-layouts  10.5 us

profile of v2, /device:TPU:0, one launch (start us, length us, event | category | flops | bytes accessed | tf_op | source)
XLA Modules:
  0.0 74.2 jit_solution(4752020958112894186)
XLA Ops:
  0.6 0.8 %copy.13.child_s = s32[2,4,3]{2,1,0:T(4,128)S(1)} copy(s32[2,4,3]{1,0,2:T(2,128)} %param.13) | data formatting | bytes 192 | tf_op args[5]
  1.4 0.0 copy-start
  1.4 1.6 %copy-done = bf16[1024,1024]{1,0:T(8,128)(2,1)S(1)} copy-done((bf16[1024,1024]{1,0:T(8,128)(2,1)S(1)}, bf16[1024,1024]{1,0:T(8,128)(2,1)}, u32[]{:S(2)}) %copy-start) | copy-done | bytes 2097176
  3.0 0.0 copy-start.1
  3.0 0.9 %copy-done.1 = bf16[1,1,6,128,128]{4,3,2,1,0:T(8,128)(2,1)S(1)} copy-done((bf16[1,1,6,128,128]{4,3,2,1,0:T(8,128)(2,1)S(1)}, bf16[1,1,6,128,128]{4,3,2,1,0:T(8,128)(2,1)}, u32[]{:S(2)}) %copy-start.1) | copy-done | bytes 196632
  3.9 0.0 copy-start.2
  3.9 0.9 %copy-done.2 = bf16[2,1,3,128,128]{4,3,2,1,0:T(8,128)(2,1)S(1)} copy-done((bf16[2,1,3,128,128]{4,3,2,1,0:T(8,128)(2,1)S(1)}, bf16[2,1,3,128,128]{4,3,2,1,0:T(8,128)(2,1)}, u32[]{:S(2)}) %copy-start.2) | copy-done | bytes 196632
  4.9 0.0 copy-start.3
  4.9 0.9 %copy-done.3 = f32[2,128,128]{2,1,0:T(8,128)S(1)} copy-done((f32[2,128,128]{2,1,0:T(8,128)S(1)}, f32[2,128,128]{2,1,0:T(8,128)}, u32[]{:S(2)}) %copy-start.3) | copy-done | bytes 131096
  5.8 0.0 copy-start.4
  5.8 0.8 %copy-done.4 = bf16[2,128,128]{2,1,0:T(8,128)(2,1)S(1)} copy-done((bf16[2,128,128]{2,1,0:T(8,128)(2,1)S(1)}, bf16[2,128,128]{2,1,0:T(8,128)(2,1)}, u32[]{:S(2)}) %copy-start.4) | copy-done | bytes 65560
  6.6 0.0 copy-start.5
  6.6 0.8 %copy-done.5 = f32[1,128,128]{2,1,0:T(8,128)S(1)} copy-done((f32[1,128,128]{2,1,0:T(8,128)S(1)}, f32[1,128,128]{2,1,0:T(8,128)}, u32[]{:S(2)}) %copy-start.5) | copy-done | bytes 65560
  7.4 0.0 copy-start.6
  7.4 0.7 copy-done.6
  8.1 63.0 %shard_map.119 = (bf16[6,128,128]{2,1,0:T(8,128)(2,1)S(1)}, f32[1,128]{1,0:T(1,128)S(1)}, bf16[6,128,128]{2,1,0:T(8,128)(2,1)S(1)}, bf16[2,128,128]{2,1,0:T(8,128)(2,1)S(1)}, f32[2,128]{1,0:T(2,128)S(1)}) custom-call(bf16[1024,1024]{1,0:T(8,128)(2,1)S(1)} %copy-done, bf16[6,128,128]{2,1,0:T(8,128)(2,1)S(1)} %bitcast.7, bf16[6,128,128]{2,1,0:T(8,128)(2,1)S(1)} %bitcast.8, ...), custom_call_target="tpu_custom_call" | custom-call | tf_op jit(solution)/shard_map/pallas_call | solution.py:618
  71.1 0.7 copy.20
  71.8 0.5 copy.21
  72.3 0.7 copy.22
  73.0 0.6 copy.23
  73.6 0.6 copy.24
Async XLA Ops:
  1.4 1.6 %copy-start = (bf16[1024,1024]{1,0:T(8,128)(2,1)S(1)}, bf16[1024,1024]{1,0:T(8,128)(2,1)}, u32[]{:S(2)}) copy-start(bf16[1024,1024]{1,0:T(8,128)(2,1)} %sig_hbm.1) | copy-start | bytes 6291460
  3.0 0.9 %copy-start.1 = (bf16[1,1,6,128,128]{4,3,2,1,0:T(8,128)(2,1)S(1)}, bf16[1,1,6,128,128]{4,3,2,1,0:T(8,128)(2,1)}, u32[]{:S(2)}) copy-start(bf16[1,1,6,128,128]{4,3,2,1,0:T(8,128)(2,1)} %param.9) | copy-start | bytes 589828
  3.9 0.9 %copy-start.2 = (bf16[2,1,3,128,128]{4,3,2,1,0:T(8,128)(2,1)S(1)}, bf16[2,1,3,128,128]{4,3,2,1,0:T(8,128)(2,1)}, u32[]{:S(2)}) copy-start(bf16[2,1,3,128,128]{4,3,2,1,0:T(8,128)(2,1)} %param.11) | copy-start | bytes 589828
  4.9 0.9 %copy-start.3 = (f32[2,128,128]{2,1,0:T(8,128)S(1)}, f32[2,128,128]{2,1,0:T(8,128)}, u32[]{:S(2)}) copy-start(f32[2,128,128]{2,1,0:T(8,128)} %cinv_hbm.1) | copy-start | bytes 393220
  5.8 0.8 %copy-start.4 = (bf16[2,128,128]{2,1,0:T(8,128)(2,1)S(1)}, bf16[2,128,128]{2,1,0:T(8,128)(2,1)}, u32[]{:S(2)}) copy-start(bf16[2,128,128]{2,1,0:T(8,128)(2,1)} %top_hbm.1) | copy-start | bytes 196612
  6.6 0.8 %copy-start.5 = (f32[1,128,128]{2,1,0:T(8,128)S(1)}, f32[1,128,128]{2,1,0:T(8,128)}, u32[]{:S(2)}) copy-start(f32[1,128,128]{2,1,0:T(8,128)} %param.14) | copy-start | bytes 196612
  7.4 0.7 copy-start.6

commit v3 on v2

--- a/solution.py
+++ b/solution.py
@@ -490,7 +490,6 @@
         pan_all[z, pl.ds(0, slots)].reshape(slots * width, width),
         pcol[...].reshape(slots * width, width),
     )
-    tail_recv[col, pl.ds(kids * width, 8)] = jnp.broadcast_to(par_diag, (8, width))
     lifted = []
     for kid in range(kids):
         selected = []
@@ -508,7 +507,7 @@
         piece = piece - jnp.dot(
             par_piece, wide_top[kid], precision=precise, preferred_element_type=jnp.float32
         )
-        tail_recv[col, pl.ds(kid * width, width)] = piece
+        tail_recv[col, pl.ds(kid * width, width)] = piece.astype(jnp.bfloat16)
         lifted.append(jnp.dot(chosen, top[kid], preferred_element_type=jnp.float32))
     send_across(1)
     send_to_columns(tail_recv, tail_send, tail_recv_sem)
@@ -532,18 +531,17 @@
                 keepdims=True,
             )
         kid_diags.append(kid_diag)
-    kid_diags.append(jnp.zeros((8 - kids, width), jnp.float32))
+    kid_diags.append(jnp.broadcast_to(par_diag, (8 - kids, width)))
     kid_recv[col] = jnp.concatenate(kid_diags, axis=0)
     send_to_columns(kid_recv, kid_send, kid_recv_sem)
 
     take_from_columns(tail_recv, tail_send, tail_recv_sem)
-    par_total = [tail_recv[c, pl.ds(kids * width, 8)][0:1] for c in range(COLS)]
-    pvar[...] = jnp.sum(pinv[...] * pinv[...], axis=0, keepdims=True) - (
-        par_total[0] + par_total[1] + par_total[2] + par_total[3]
-    )
+    par_squares = jnp.sum(pinv[...] * pinv[...], axis=0, keepdims=True)
     known = []
     for kid in range(kids):
-        part = [tail_recv[c, pl.ds(kid * width, width)] for c in range(COLS)]
+        part = [
+            tail_recv[c, pl.ds(kid * width, width)].astype(jnp.float32) for c in range(COLS)
+        ]
         rows = part[0] + part[1] + part[2] + part[3] + gram_top[kid]
         crow[kid] = (-rows).astype(jnp.bfloat16)
         inv = cinv[kid]
@@ -553,6 +551,7 @@
         )
     take_from_columns(kid_recv, kid_send, kid_recv_sem)
     kid_total = kid_recv[0] + kid_recv[1] + kid_recv[2] + kid_recv[3]
+    pvar[...] = par_squares - kid_total[kids : kids + 1]
     for kid in range(kids):
         cvar[pl.ds(kid, 1), :] = known[kid] - kid_total[kid : kid + 1]
 
@@ -636,7 +635,7 @@
             pltpu.VMEM((ROWS, COLS, blocks + pad, LANES), bf16),
             pltpu.VMEM((group_blocks * width, (1 + kids) * width), bf16),
             pltpu.VMEM((group_blocks * width, (1 + kids) * width), f32),
-            pltpu.VMEM((COLS, kids * width + 8, width), f32),
+            pltpu.VMEM((COLS, kids * width, width), bf16),
             pltpu.VMEM((COLS, 8, width), f32),
             pltpu.VMEM(sigma_top.shape, bf16),
             pltpu.VMEM(child_top.shape, bf16),
@@ -660,7 +659,7 @@
             dma((COLS,)),
         ],
         compiler_params=pltpu.CompilerParams(
-            collective_id=0, has_side_effects=True, vmem_limit_bytes=40 * 1024 * 1024
+            collective_id=0, has_side_effects=True, vmem_limit_bytes=60 * 1024 * 1024
         ),
     )(
         sigma_top,

time: 75.2 us -> 71.9 us (0.956)
  local copies, waits for them, and re-layouts: 10.5 us -> 8.44 us
    unnamed x20 -> x6, local copies, waits for them, and re-layouts: 10.5 us -> 8.44 us
where the time goes in v3:
time: 71.9 us; the launch traced here: 71.6 us
  Pallas kernels  62.5 us (87%)
  local copies, waits for them, and re-layouts  8.44 us (12%)
    pallas_call x1, Pallas kernels, on_device_kernel(): pl.pallas_call(functools.partial(fused_kernel, slots, picks, kids), out_s...  62.5 us
    unnamed x6, local copies, waits for them, and re-layouts  8.44 us

profile of v3, /device:TPU:0, one launch (start us, length us, event | category | flops | bytes accessed | tf_op | source)
XLA Modules:
  0.0 71.6 jit_solution(9539876519904341664)
XLA Ops:
  0.6 1.4 %copy.13.child_s = s32[2,4,3]{2,1,0:T(4,128)} copy(s32[2,4,3]{1,0,2:T(2,128)} %param.13) | data formatting | bytes 192 | tf_op args[5]
  2.0 62.5 %shard_map.119 = (bf16[6,128,128]{2,1,0:T(8,128)(2,1)}, f32[1,128]{1,0:T(1,128)}, bf16[6,128,128]{2,1,0:T(8,128)(2,1)}, bf16[2,128,128]{2,1,0:T(8,128)(2,1)}, f32[2,128]{1,0:T(2,128)}) custom-call(bf16[1024,1024]{1,0:T(8,128)(2,1)} %sig_hbm.1, bf16[6,128,128]{2,1,0:T(8,128)(2,1)} %bitcast.7, bf16[6,128,128]{2,1,0:T(8,128)(2,1)} %bitcast.8, ...), custom_call_target="tpu_custom_call" | custom-call | tf_op jit(solution)/shard_map/pallas_call | solution.py:617
  64.5 1.6 %copy.20 = bf16[1,1,6,128,128]{4,3,2,1,0:T(8,128)(2,1)} copy(bf16[1,1,6,128,128]{4,3,2,1,0:T(8,128)(2,1)} %bitcast.10) | data formatting | bytes 393216
  66.2 1.1 %copy.21 = f32[1,128]{1,0:T(1,128)} copy(f32[1,128]{1,0:T(1,128)} %get-tuple-element.26) | data formatting | bytes 1024
  67.3 1.6 %copy.22 = bf16[2,1,3,128,128]{4,3,2,1,0:T(8,128)(2,1)} copy(bf16[2,1,3,128,128]{4,3,2,1,0:T(8,128)(2,1)} %bitcast.9) | data formatting | bytes 393216
  68.9 1.5 %copy.23 = bf16[2,128,128]{2,1,0:T(8,128)(2,1)} copy(bf16[2,128,128]{2,1,0:T(8,128)(2,1)} %get-tuple-element.28) | data formatting | bytes 131072
  70.4 1.2 %copy.24 = f32[2,128]{1,0:T(2,128)} copy(f32[2,128]{1,0:T(2,128)} %get-tuple-element.29) | data formatting | bytes 2048

commit v4 on v3

--- a/solution.py
+++ b/solution.py
@@ -281,7 +281,9 @@
         list_copy(step).start()
     loads[0].wait()
     send_own(0)
-    for load in loads[1:]:
+    loads[1].wait()
+    send_own(1)
+    for load in loads[2:]:
         load.wait()
 
     def cut(ref, index, part):
@@ -425,12 +427,6 @@
 
                     if part == 0:
                         list_arrival(p).wait_recv()
-
-                if part == 0:
-
-                    @pl.when(t == 1)
-                    def _():
-                        send_own(1)
 
                 compute(p, part)
 

time: 71.9 us -> 71.5 us (level)
  no operation moved by 1% of the time
where the time goes in v4:
time: 71.5 us; the launch traced here: 71.2 us
  Pallas kernels  62.1 us (87%)
  local copies, waits for them, and re-layouts  8.44 us (12%)
    pallas_call x1, Pallas kernels, on_device_kernel(): pl.pallas_call(functools.partial(fused_kernel, slots, picks, kids), out_s...  62.1 us
    unnamed x6, local copies, waits for them, and re-layouts  8.44 us

profile of v4, /device:TPU:0, one launch (start us, length us, event | category | flops | bytes accessed | tf_op | source)
XLA Modules:
  0.0 71.2 jit_solution(6053182108730823640)
XLA Ops:
  0.6 1.4 %copy.13.child_s = s32[2,4,3]{2,1,0:T(4,128)} copy(s32[2,4,3]{1,0,2:T(2,128)} %param.13) | data formatting | bytes 192 | tf_op args[5]
  2.0 62.1 %shard_map.119 = (bf16[6,128,128]{2,1,0:T(8,128)(2,1)}, f32[1,128]{1,0:T(1,128)}, bf16[6,128,128]{2,1,0:T(8,128)(2,1)}, bf16[2,128,128]{2,1,0:T(8,128)(2,1)}, f32[2,128]{1,0:T(2,128)}) custom-call(bf16[1024,1024]{1,0:T(8,128)(2,1)} %sig_hbm.1, bf16[6,128,128]{2,1,0:T(8,128)(2,1)} %bitcast.7, bf16[6,128,128]{2,1,0:T(8,128)(2,1)} %bitcast.8, ...), custom_call_target="tpu_custom_call" | custom-call | tf_op jit(solution)/shard_map/pallas_call | solution.py:613
  64.1 1.6 %copy.20 = bf16[1,1,6,128,128]{4,3,2,1,0:T(8,128)(2,1)} copy(bf16[1,1,6,128,128]{4,3,2,1,0:T(8,128)(2,1)} %bitcast.10) | data formatting | bytes 393216
  65.7 1.1 %copy.21 = f32[1,128]{1,0:T(1,128)} copy(f32[1,128]{1,0:T(1,128)} %get-tuple-element.26) | data formatting | bytes 1024
  66.8 1.6 %copy.22 = bf16[2,1,3,128,128]{4,3,2,1,0:T(8,128)(2,1)} copy(bf16[2,1,3,128,128]{4,3,2,1,0:T(8,128)(2,1)} %bitcast.9) | data formatting | bytes 393216
  68.4 1.5 %copy.23 = bf16[2,128,128]{2,1,0:T(8,128)(2,1)} copy(bf16[2,128,128]{2,1,0:T(8,128)(2,1)} %get-tuple-element.28) | data formatting | bytes 131072
  69.9 1.2 %copy.24 = f32[2,128]{1,0:T(2,128)} copy(f32[2,128]{1,0:T(2,128)} %get-tuple-element.29) | data formatting | bytes 2048
